TPU v7x, 32 devices: a whole 2x2x4 slice. The times are simulated.
32 devices in a mesh: groups: 2 (over x), dap: 8 (over z, y), rep: 2 (over core).
Axes of the slice: x: 2, y: 2, z: 4, core: 2. Of those that a mesh axis runs over, the one named last changes fastest.
Arguments:
- pair_input: bfloat16 [128, 64, 128], P(('groups', 'dap')), parts along dimension 0, may hold values from -6 to 6
- outgoing_weights: bfloat16 [4, 128, 128], P(None, None, 'rep'), may hold values from -0.5 to 0.5
- outgoing_gate: bfloat16 [128, 128], P(None, 'rep'), may hold values from -0.5 to 0.5
- outgoing_output: bfloat16 [128, 128], P('rep'), may hold values from -0.5 to 0.5
- incoming_weights: bfloat16 [4, 128, 128], P(None, None, 'rep'), may hold values from -0.5 to 0.5
- incoming_gate: bfloat16 [128, 128], P(None, 'rep'), may hold values from -0.5 to 0.5
- incoming_output: bfloat16 [128, 128], P('rep'), may hold values from -0.5 to 0.5
- distogram_head: bfloat16 [128, 64], replicated, may hold values from -0.5 to 0.5
- distance_bins: int32 [128, 64], P('groups'), parts along dimension 0, may hold values from 0 to 63
- chain_index: int32 [128], P('groups'), parts along dimension 0, may hold values from 0 to 7, as said below
- chain_swap: int32 [16], P('groups'), parts along dimension 0, may hold values from 0 to 7, as said below
Outputs:
- pair_grad: float32 [128, 64, 128], P(('groups', 'dap')), parts along dimension 0
- grad_outgoing_weights: float32 [8, 128, 128], P('groups', None, 'rep'), parts along dimension 0
- grad_outgoing_gate: float32 [256, 128], P('groups', 'rep'), parts along dimension 0
- grad_outgoing_output: float32 [256, 128], P(('groups', 'rep')), parts along dimension 0
- grad_incoming_weights: float32 [8, 128, 128], P('groups', None, 'rep'), parts along dimension 0
- grad_incoming_gate: float32 [256, 128], P('groups', 'rep'), parts along dimension 0
- grad_incoming_output: float32 [256, 128], P(('groups', 'rep')), parts along dimension 0
- grad_distogram_head: float32 [256, 64], P('groups'), parts along dimension 0
There are 2 independent parts, one for each index of `groups`. A program takes and returns all parts, laid end to end along the dimension named above; an argument that names none is the same for every part. Nothing has to cross between parts.
Inputs may be any that keep to these rules, and one draw needn't show every extreme that they name: `chain_index`: never falls; every chain has at least one residue; chains 2m and 2m + 1 have equal lengths. `chain_swap`: A permutation of the chains that maps chain 2m to 2m or 2m + 1 and chain 2m + 1 to the other one.
All inputs are finite; a program needn't handle non-finite values.
Results may differ from a plain program's by a relative error of at most 0.025.
Values may be sent and summed in bfloat16 or wider, within the bound.
A program may use at most 192 MiB of HBM per device.

v0:
```python
import jax
import jax.numpy as jnp
from jax import lax
from jax.sharding import PartitionSpec as P

H = 128


epsilon = 1e-05


def normalize(values):
    center = jnp.mean(values, axis=-1, keepdims=True)
    centred = values - center
    inverse = lax.rsqrt(jnp.mean(centred * centred, axis=-1, keepdims=True) + epsilon)
    return (centred * inverse, inverse)


def triangle_forward(pair_rows, weights, gate_w, out_w, roles):
    value_left, gate_left, value_right, gate_right = roles
    pair_float = pair_rows.astype(jnp.float32)
    pair_hat, pair_inverse = normalize(pair_float)
    normed = pair_hat.astype(jnp.bfloat16)
    projected = jnp.einsum("rnc,qch->qhrn", normed, weights, preferred_element_type=jnp.float32)
    local_side = (jax.nn.sigmoid(projected[gate_left]) * projected[value_left]).astype(jnp.bfloat16)
    remote_side = (jax.nn.sigmoid(projected[gate_right]) * projected[value_right]).astype(
        jnp.bfloat16
    )
    remote_all = lax.all_gather(remote_side, "dap", axis=1, tiled=True)
    mixed_sum = jnp.einsum(
        "hik,hjk->hij", local_side, remote_all, preferred_element_type=jnp.float32
    )
    total_one, total_two = lax.psum(
        (jnp.sum(mixed_sum, axis=0), jnp.sum(mixed_sum * mixed_sum, axis=0)), "rep"
    )
    mean_hidden = total_one / H
    inv_hidden = lax.rsqrt(total_two / H - mean_hidden * mean_hidden + epsilon)
    mixed_hat = (mixed_sum - mean_hidden) * inv_hidden
    mixed_norm = mixed_hat.astype(jnp.bfloat16)
    partial_out = jnp.einsum("hrn,hc->rnc", mixed_norm, out_w, preferred_element_type=jnp.float32)
    update_half = lax.psum_scatter(partial_out, "rep", scatter_dimension=2, tiled=True)
    gating = jax.nn.sigmoid(
        jnp.einsum("rnc,cd->rnd", normed, gate_w, preferred_element_type=jnp.float32)
    )
    update_full = lax.all_gather(gating * update_half, "rep", axis=2, tiled=True)
    result = (pair_float + update_full).astype(jnp.bfloat16)
    stored = (
        pair_hat,
        pair_inverse,
        normed,
        projected,
        local_side,
        remote_all,
        mixed_hat,
        inv_hidden,
        mixed_norm,
        update_half,
        gating,
    )
    return (result, stored)


def triangle_backward(grad_out, stored, weights, gate_w, out_w, roles):
    (
        pair_hat,
        pair_inverse,
        normed,
        projected,
        local_side,
        carried,
        mixed_hat,
        inv_hidden,
        mixed_norm,
        update_half,
        gating,
    ) = stored
    value_left, gate_left, value_right, gate_right = roles
    width_half = gate_w.shape[1]
    rep_index = lax.axis_index("rep")
    grad_half = lax.dynamic_slice_in_dim(grad_out, rep_index * width_half, width_half, 2)
    grad_gate = (grad_half * update_half * gating * (1.0 - gating)).astype(jnp.bfloat16)
    update_grad_half = (grad_half * gating).astype(jnp.bfloat16)
    grad_update = lax.all_gather(update_grad_half, "rep", axis=2, tiled=True)
    d_gate = jnp.einsum("rnc,rnd->cd", normed, grad_gate, preferred_element_type=jnp.float32)
    d_output = jnp.einsum(
        "hrn,rnc->hc", mixed_norm, grad_update, preferred_element_type=jnp.float32
    )
    grad_norm = jnp.einsum("rnc,hc->hrn", grad_update, out_w, preferred_element_type=jnp.float32)
    sum_one, sum_two = lax.psum(
        (jnp.sum(grad_norm, axis=0), jnp.sum(grad_norm * mixed_hat, axis=0)), "rep"
    )
    grad_mixed = (inv_hidden * (grad_norm - sum_one / H - mixed_hat * (sum_two / H))).astype(
        jnp.bfloat16
    )
    grad_local = jnp.einsum("hij,hjk->hik", grad_mixed, carried, preferred_element_type=jnp.float32)
    swapped = lax.psum_scatter(
        jnp.einsum(
            "hij,hik->jhk", grad_mixed, local_side, preferred_element_type=jnp.float32
        ).astype(jnp.bfloat16),
        "dap",
        scatter_dimension=0,
        tiled=True,
    ).astype(jnp.float32)
    grad_remote = jnp.swapaxes(swapped, 0, 1)
    sigmoid_left = jax.nn.sigmoid(projected[gate_left])
    sigmoid_right = jax.nn.sigmoid(projected[gate_right])
    pieces = [None, None, None, None]
    pieces[value_left] = grad_local * sigmoid_left
    pieces[gate_left] = grad_local * projected[value_left] * sigmoid_left * (1.0 - sigmoid_left)
    pieces[value_right] = grad_remote * sigmoid_right
    pieces[gate_right] = (
        grad_remote * projected[value_right] * sigmoid_right * (1.0 - sigmoid_right)
    )
    grad_proj = jnp.stack(pieces).astype(jnp.bfloat16)
    d_weights = jnp.einsum("rnc,qhrn->qch", normed, grad_proj, preferred_element_type=jnp.float32)
    partial_sum = jnp.einsum(
        "qhrn,qch->rnc", grad_proj, weights, preferred_element_type=jnp.float32
    )
    partial_sum = partial_sum + jnp.einsum(
        "rnd,cd->rnc", grad_gate, gate_w, preferred_element_type=jnp.float32
    )
    grad_normed = lax.psum(partial_sum.astype(jnp.bfloat16), "rep").astype(jnp.float32)
    grad_in = grad_out + pair_inverse * (
        grad_normed
        - jnp.mean(grad_normed, axis=-1, keepdims=True)
        - pair_hat * jnp.mean(grad_normed * pair_hat, axis=-1, keepdims=True)
    )
    return (grad_in, d_weights, d_gate, d_output)


def residue_permutation(chain_index, chain_swap):
    chains = chain_swap.shape[0]
    chain_ids = jnp.arange(chains, dtype=jnp.int32)
    starts = jnp.sum((chain_index[None, :] < chain_ids[:, None]).astype(jnp.int32), axis=1)
    mapped_starts = jnp.sum(
        (chain_swap[:, None] == chain_ids[None, :]).astype(jnp.int32) * starts[None, :], axis=1
    )
    member = (chain_index[:, None] == chain_ids[None, :]).astype(jnp.int32)
    own_start = jnp.sum(member * starts[None, :], axis=1)
    new_start = jnp.sum(member * mapped_starts[None, :], axis=1)
    positions = jnp.arange(chain_index.shape[0], dtype=jnp.int32)
    return positions - own_start + new_start


def per_device(
    pair_input,
    outgoing_weights,
    outgoing_gate,
    outgoing_output,
    incoming_weights,
    incoming_gate,
    incoming_output,
    distogram_head,
    distance_bins,
    chain_index,
    chain_swap,
):
    row_count = pair_input.shape[0]
    residues = pair_input.shape[1]
    middle, stored_out = triangle_forward(
        pair_input, outgoing_weights, outgoing_gate, outgoing_output, (0, 1, 2, 3)
    )
    middle_t = jnp.swapaxes(
        lax.all_to_all(middle, "dap", split_axis=1, concat_axis=0, tiled=True), 0, 1
    )
    final_t, stored_in = triangle_forward(
        middle_t, incoming_weights, incoming_gate, incoming_output, (2, 3, 0, 1)
    )
    final_rows = jnp.swapaxes(
        lax.all_to_all(final_t, "dap", split_axis=1, concat_axis=0, tiled=True), 0, 1
    )
    half_rows = row_count // lax.axis_size("rep")
    rep_index = lax.axis_index("rep")
    own_rows = lax.dynamic_slice_in_dim(final_rows, rep_index * half_rows, half_rows, 0)
    own_cols = lax.dynamic_slice_in_dim(final_t, rep_index * half_rows, half_rows, 0)
    two_views = jnp.stack([own_rows, own_cols])
    view_logits = jnp.einsum(
        "srnc,cb->srnb", two_views, distogram_head, preferred_element_type=jnp.float32
    )
    logits = view_logits[0] + view_logits[1]
    permuted = residue_permutation(chain_index, chain_swap)
    row_ids = (
        lax.axis_index("dap") * row_count
        + rep_index * half_rows
        + jnp.arange(half_rows, dtype=jnp.int32)
    )
    target = jnp.take(
        jnp.take(distance_bins, jnp.take(permuted, row_ids), axis=0), permuted, axis=1
    )
    log_total = jnp.log(jnp.sum(jnp.exp(logits), axis=-1, keepdims=True))
    bins = distogram_head.shape[1]
    onehot = (target[:, :, None] == jnp.arange(bins, dtype=jnp.int32)[None, None, :]).astype(
        jnp.float32
    )
    grad_logits = (jnp.exp(logits - log_total) - onehot).astype(jnp.bfloat16)
    d_head = jnp.einsum("srnc,rnb->cb", two_views, grad_logits, preferred_element_type=jnp.float32)
    grad_half = jnp.einsum(
        "rnb,cb->rnc", grad_logits, distogram_head, preferred_element_type=jnp.float32
    )
    grad_rows = lax.all_gather(grad_half.astype(jnp.bfloat16), "rep", axis=0, tiled=True).astype(
        grad_half.dtype
    )
    mirrored = jnp.swapaxes(
        lax.all_to_all(
            grad_rows.astype(jnp.bfloat16), "dap", split_axis=1, concat_axis=0, tiled=True
        ).astype(grad_rows.dtype),
        0,
        1,
    )
    grad_t = grad_rows + mirrored
    grad_mid_t, dw_in, dg_in, do_in = triangle_backward(
        grad_t, stored_in, incoming_weights, incoming_gate, incoming_output, (2, 3, 0, 1)
    )
    grad_mid = jnp.swapaxes(
        lax.all_to_all(
            grad_mid_t.astype(jnp.bfloat16), "dap", split_axis=1, concat_axis=0, tiled=True
        ).astype(grad_mid_t.dtype),
        0,
        1,
    )
    pair_grad, dw_out, dg_out, do_out = triangle_backward(
        grad_mid, stored_out, outgoing_weights, outgoing_gate, outgoing_output, (0, 1, 2, 3)
    )
    grad_sums = (
        lax.psum(dw_out.astype(jnp.bfloat16), "dap").astype(jnp.float32),
        lax.psum(dg_out.astype(jnp.bfloat16), "dap").astype(jnp.float32),
        lax.psum(do_out.astype(jnp.bfloat16), "dap").astype(jnp.float32),
        lax.psum(dw_in.astype(jnp.bfloat16), "dap").astype(jnp.float32),
        lax.psum(dg_in.astype(jnp.bfloat16), "dap").astype(jnp.float32),
        lax.psum(do_in.astype(jnp.bfloat16), "dap").astype(jnp.float32),
    )
    head_total = lax.psum(d_head, ("dap", "rep"))
    inv_count = 1.0 / residues
    return (
        pair_grad,
        grad_sums[0] * inv_count,
        grad_sums[1] * inv_count,
        grad_sums[2] * inv_count,
        grad_sums[3] * inv_count,
        grad_sums[4] * inv_count,
        grad_sums[5] * inv_count,
        head_total * inv_count,
    )


def solution(mesh):
    return jax.shard_map(
        per_device,
        mesh=mesh,
        in_specs=(
            P(("groups", "dap"), None, None),
            P(None, None, "rep"),
            P(None, "rep"),
            P("rep", None),
            P(None, None, "rep"),
            P(None, "rep"),
            P("rep", None),
            P(),
            P("groups", None),
            P("groups"),
            P("groups"),
        ),
        out_specs=(
            P(("groups", "dap"), None, None),
            P("groups", None, "rep"),
            P("groups", "rep"),
            P(("groups", "rep"), None),
            P("groups", None, "rep"),
            P("groups", "rep"),
            P(("groups", "rep"), None),
            P("groups", None),
        ),
        check_vma=False,
    )
```

profile of v0, /device:TPU:0, one launch (start us, length us, event | category | flops | bytes accessed | tf_op | source)
XLA Modules:
  0.0 557.1 jit_solution(51799186579937044)
XLA Ops:
  7.2 1.1 convert_reduce_fusion.2
  9.8 34.6 %all_gather.21 = bf16[64,64,64]{2,0,1:T(8,128)(2,1)S(1)} all-gather(bf16[64,8,64]{2,0,1:T(8,128)(2,1)S(1)} %copy.147), channel_id=1, replica_groups=mesh['groups'=2,'dap'=8,'rep'=2] {'dap'}, dimensions={1}, use_global_device_ids=true | all-gather | bytes 589824 | tf_op jit(solution)/shard_map/all_gather | solution.py:29
  45.4 2.5 all-reduce.3
  53.8 5.4 reduce-scatter.13.cloned.1.call-done
  59.2 1.0 reshape.259
  60.9 1.0 fusion.152
  62.1 2.2 all_gather.22
  65.3 5.9 %all-to-all-start = ((bf16[8,64,128]{2,0,1:T(8,128)(2,1)}), bf16[8,64,128]{2,0,1:T(8,128)(2,1)S(1)}, u32[]{:S(2)}, u32[]{:S(2)}) async-start(bf16[8,64,128]{2,0,1:T(8,128)(2,1)} %copy.153), calls=%async_computation | async-start | bytes 262144 | tf_op jit(solution)/shard_map/all_to_all | solution.py:164
  71.8 6.8 %all-to-all-done = bf16[8,64,128]{2,0,1:T(8,128)(2,1)S(1)} async-done(((bf16[8,64,128]{2,0,1:T(8,128)(2,1)}), bf16[8,64,128]{2,0,1:T(8,128)(2,1)S(1)}, u32[]{:S(2)}, u32[]{:S(2)}) %all-to-all-start) | async-done | bytes 131104 | tf_op jit(solution)/shard_map/all_to_all | solution.py:164
  80.6 1.7 copy.156
  82.3 35.0 %all_gather.23 = bf16[64,64,64]{2,0,1:T(8,128)(2,1)} all-gather(bf16[64,8,64]{2,0,1:T(8,128)(2,1)} %copy.156), channel_id=1, replica_groups=mesh['groups'=2,'dap'=8,'rep'=2] {'dap'}, dimensions={1}, use_global_device_ids=true | all-gather | bytes 589824 | tf_op jit(solution)/shard_map/all_gather | solution.py:29
  117.3 1.7 copy.157
  119.0 2.8 fusion.150
  121.8 2.5 all-reduce.2
  124.3 1.0 fusion.90
  126.9 1.9 copy.209
  128.8 1.9 reshape.260
  132.8 3.8 reduce-scatter.15.cloned.1.call-done
  136.6 1.7 reshape.261
  138.3 1.8 copy.210
  140.1 2.1 fusion.153
  142.2 1.8 copy.160
  144.0 5.1 all_gather.24
  149.1 1.9 copy.161
  153.4 5.9 %all-to-all-start.1 = ((bf16[8,64,128]{2,0,1:T(8,128)(2,1)}), bf16[8,64,128]{2,0,1:T(8,128)(2,1)}, u32[]{:S(2)}, u32[]{:S(2)}) async-start(bf16[8,64,128]{2,0,1:T(8,128)(2,1)} %copy.162), calls=%async_computation.1 | async-start | bytes 262144 | tf_op jit(solution)/shard_map/all_to_all | solution.py:170
  161.6 5.2 all-to-all-done.1
  169.4 2.0 convolution_convert_fusion
  171.4 2.1 all_gather.25
  174.9 4.0 all-to-all-start.2
  179.0 7.5 %all-to-all-done.2 = bf16[8,64,128]{2,0,1:T(8,128)(2,1)} async-done(((bf16[8,64,128]{2,0,1:T(8,128)(2,1)}), bf16[8,64,128]{2,0,1:T(8,128)(2,1)}, u32[]{:S(2)}, u32[]{:S(2)}) %all-to-all-start.2) | async-done | bytes 131104 | tf_op jit(solution)/shard_map/all_to_all | solution.py:204
  186.5 1.1 bitcast_add_fusion
  188.5 1.7 copy.169
  190.2 3.5 all_gather.26
  193.7 1.8 copy.170
  195.5 1.2 fusion.126
  197.5 3.2 all-reduce.1
  201.4 1.2 fusion.81
  203.3 1.5 fusion.154
  204.8 4.0 copy.173
  208.9 1.5 convert_reduce_fusion.3
  210.4 1.4 convolution_bitcast_fusion.6
  211.7 59.6 %psum.135 = f32[128,64]{0,1:T(8,128)S(1)} all-reduce(f32[128,64]{0,1:T(8,128)S(1)} %convolution_bitcast_fusion.6), channel_id=1, replica_groups=mesh['groups'=2,'dap'=8,'rep'=2] {'dap','rep'}, use_global_device_ids=true, to_apply=%region_42.43 | all-reduce | flops 8192 | bytes 65536 | tf_op jit(solution)/shard_map/psum | solution.py:232
  271.9 2.8 fusion.22
  274.7 1.8 copy.175
  276.5 1.3 fusion.99
  280.7 13.8 %all-reduce.11.cloned.1.call-done = bf16[8,64,128]{2,1,0:T(8,128)(2,1)} async-done(((bf16[8,64,128]{2,1,0:T(8,128)(2,1)}), bf16[8,64,128]{2,1,0:T(8,128)(2,1)}) %all-reduce.11.cloned.1.call-update) | async-done | bytes 131088 | tf_op jit(solution)/shard_map/psum | solution.py:122
  294.5 1.3 convert_reduce_fusion.1
  297.0 5.9 %all-to-all-start.3 = ((bf16[8,64,128]{2,0,1:T(8,128)(2,1)}), bf16[8,64,128]{2,0,1:T(8,128)(2,1)S(1)}, u32[]{:S(2)}, u32[]{:S(2)}) async-start(bf16[8,64,128]{2,0,1:T(8,128)(2,1)} %copy.177), calls=%async_computation.4 | async-start | bytes 262144 | tf_op jit(solution)/shard_map/all_to_all | solution.py:215
  303.9 2.0 fusion.16
  305.9 4.4 all-to-all-done.3
  310.7 2.0 all_gather.27
  316.5 2.5 all-reduce
  319.9 1.5 fusion.155
  321.4 2.9 copy.186
  326.1 61.4 %all-reduce.15.cloned.1.call-done = (bf16[128,64]{0,1:T(8,128)(2,1)}, bf16[64,128]{1,0:T(8,128)(2,1)}, bf16[128,64]{0,1:T(8,128)(2,1)}, bf16[64,128]{1,0:T(8,128)(2,1)}) async-done(((bf16[128,64]{0,1:T(8,128)(2,1)}, bf16[64,128]{1,0:T(8,128)(2,1)}, bf16[128,64]{0,1:T(8,128)(2,1)}, bf16[64,128]{1,0:T(8,128)(2,1)}), (bf16[128,64]{0,1:T(8,128)(2,1)}, bf16[64,128]{1,0:T(8,128)(2,1)}, bf16[128,64]{0,1:T(8,128)(2,1)}, ...) | async-done | bytes 65552 | tf_op jit(solution)/shard_map/psum | solution.py:226
  387.6 1.3 convert_multiply_fusion.4
  391.0 63.7 %reduce-scatter.11.cloned.1.call-done = bf16[8,64,64]{1,2,0:T(8,128)(2,1)} async-done(((bf16[64,64,64]{1,2,0:T(8,128)(2,1)}), bf16[8,64,64]{1,2,0:T(8,128)(2,1)}) %reduce-scatter.11.cloned.1.call-update) | async-done | bytes 65552 | tf_op jit(solution)/shard_map/reduce_scatter | solution.py:96
  454.6 1.2 fusion.96
  455.8 1.1 fusion.17
  459.0 68.6 %all-reduce.17.cloned.1.call-done = (bf16[4,128,64]{1,2,0:T(8,128)(2,1)}, bf16[4,128,64]{1,2,0:T(8,128)(2,1)}) async-done(((bf16[4,128,64]{1,2,0:T(8,128)(2,1)}, bf16[4,128,64]{1,2,0:T(8,128)(2,1)}), (bf16[4,128,64]{1,2,0:T(8,128)(2,1)}, bf16[4,128,64]{1,2,0:T(8,128)(2,1)})) %all-reduce.17.cloned.1.call-update) | async-done | bytes 131088 | tf_op jit(solution)/shard_map/psum | solution.py:225
  527.6 1.5 convert_multiply_fusion.2
  529.8 18.0 %all-reduce.13.cloned.1.call-done = bf16[8,64,128]{2,1,0:T(8,128)(2,1)} async-done(((bf16[8,64,128]{2,1,0:T(8,128)(2,1)}), bf16[8,64,128]{2,1,0:T(8,128)(2,1)}) %all-reduce.13.cloned.1.call-update) | async-done | bytes 131088 | tf_op jit(solution)/shard_map/psum | solution.py:122
  547.8 1.3 convert_reduce_fusion
  549.2 1.0 fusion.36
  (244 shorter events, 45.3 us)
Async XLA Ops:
  7.2 72.2 %copy-start = (bf16[4,128,64]{1,2,0:T(8,128)(2,1)S(1)}, bf16[4,128,64]{1,2,0:T(8,128)(2,1)}, u32[]{:S(2)}) copy-start(bf16[4,128,64]{1,2,0:T(8,128)(2,1)} %param.15) | copy-start | bytes 196612
  7.2 1.2 copy-start.1
  7.2 52.0 %reduce-scatter.13.cloned.1.call-start = ((), (), s32[]{:S(2)}) async-start(), calls=%async_computation.12 | async-start | bytes 393216
  8.3 0.8 copy-start.49
  44.6 0.8 copy-start.16
  45.4 4.0 copy-start.4
  47.9 1.3 copy-start.53
  60.2 0.7 copy-start.58
  60.9 1.0 copy-start.20
  65.3 5.9 %copy-start.63 = (s32[64,64]{1,0:T(8,128)S(1)}, s32[64,64]{1,0:T(8,128)}, u32[]{:S(2)}) copy-start(s32[64,64]{1,0:T(8,128)} %param.19) | copy-start | bytes 49156
  65.3 13.4 %all-to-all-start = ((bf16[8,64,128]{2,0,1:T(8,128)(2,1)}), bf16[8,64,128]{2,0,1:T(8,128)(2,1)S(1)}, u32[]{:S(2)}, u32[]{:S(2)}) async-start(bf16[8,64,128]{2,0,1:T(8,128)(2,1)} %copy.153), calls=%async_computation | async-start | bytes 262144 | tf_op jit(solution)/shard_map/all_to_all | solution.py:164
  71.2 65.4 %reduce-scatter.15.cloned.1.call-start = ((), (), s32[]{:S(2)}) async-start(), calls=%async_computation.13 | async-start | bytes 393216
  124.3 1.0 copy-start.43
  124.3 1.0 copy-start.46
  124.3 1.7 copy-start.52
  138.3 1.8 copy-start.56
  153.4 13.4 %all-to-all-start.1 = ((bf16[8,64,128]{2,0,1:T(8,128)(2,1)}), bf16[8,64,128]{2,0,1:T(8,128)(2,1)}, u32[]{:S(2)}, u32[]{:S(2)}) async-start(bf16[8,64,128]{2,0,1:T(8,128)(2,1)} %copy.162), calls=%async_computation.1 | async-start | bytes 262144 | tf_op jit(solution)/shard_map/all_to_all | solution.py:170
  167.7 0.7 copy-start.55
  174.9 11.6 %all-to-all-start.2 = ((bf16[8,64,128]{2,0,1:T(8,128)(2,1)}), bf16[8,64,128]{2,0,1:T(8,128)(2,1)}, u32[]{:S(2)}, u32[]{:S(2)}) async-start(bf16[8,64,128]{2,0,1:T(8,128)(2,1)} %copy.167), calls=%async_computation.2 | async-start | bytes 262144 | tf_op jit(solution)/shard_map/all_to_all | solution.py:204
  178.9 97.6 %reduce-scatter.9.cloned.1.call-start = ((), (), s32[]{:S(2)}) async-start(), calls=%async_computation.8 | async-start | bytes 1179648 | tf_op jit(solution)/shard_map/reduce_scatter | solution.py:96
  186.5 1.1 copy-start.22
  186.5 1.2 copy-start.31
  187.6 0.9 copy-start.8
  195.5 1.2 copy-start.6
  195.5 1.2 copy-start.44
  195.5 1.2 copy-start.47
  196.7 0.8 copy-start.7
  200.7 0.7 copy-start.45
  200.7 0.7 copy-start.48
  201.4 1.9 copy-start.17
  208.8 85.7 %all-reduce.11.cloned.1.call-start = ((), (), s32[]{:S(2)}) async-start(), calls=%async_computation.9 | async-start | bytes 262144 | tf_op jit(solution)/shard_map/psum | solution.py:122
  277.8 0.7 copy-start.34
  277.8 0.7 copy-start.36
  277.8 0.8 copy-start.38
  277.8 1.1 copy-start.29
  277.8 1.0 copy-start.57
  279.7 14.8 %copy-start.3 = (f32[8,8,8,128]{3,0,2,1:T(8,128)S(1)}, f32[8,8,8,128]{3,0,2,1:T(8,128)}, u32[]{:S(2)}) copy-start(f32[8,8,8,128]{3,0,2,1:T(8,128)} %copy-done.2) | copy-start | bytes 786436
  280.7 15.2 %copy-start.9 = (f32[8,64,128]{2,1,0:T(8,128)S(1)}, f32[8,64,128]{2,1,0:T(8,128)}, u32[]{:S(2)}) copy-start(f32[8,64,128]{2,1,0:T(8,128)} %copy-done.8) | copy-start | bytes 786436
  294.5 1.4 copy-start.25
  296.2 7.6 %copy-start.37 = (bf16[1,64,8,64]{1,3,2,0:T(8,128)(2,1)S(1)}, bf16[1,64,8,64]{1,3,2,0:T(8,128)(2,1)}, u32[]{:S(2)}) copy-start(bf16[1,64,8,64]{1,3,2,0:T(8,128)(2,1)} %copy-done.36) | copy-start | bytes 196612
  297.0 6.0 %copy-start.13 = (bf16[64,8,64]{2,1,0:T(8,128)(2,1)S(1)}, bf16[64,8,64]{2,1,0:T(8,128)(2,1)}, u32[]{:S(2)}) copy-start(bf16[64,8,64]{2,1,0:T(8,128)(2,1)} %copy-done.12) | copy-start | bytes 196612
  297.0 6.0 %copy-start.14 = (bf16[8,64,128]{2,1,0:T(8,128)(2,1)S(1)}, bf16[8,64,128]{2,1,0:T(8,128)(2,1)}, u32[]{:S(2)}) copy-start(bf16[8,64,128]{2,1,0:T(8,128)(2,1)} %copy.170) | copy-start | bytes 393220
  297.0 13.4 %all-to-all-start.3 = ((bf16[8,64,128]{2,0,1:T(8,128)(2,1)}), bf16[8,64,128]{2,0,1:T(8,128)(2,1)S(1)}, u32[]{:S(2)}, u32[]{:S(2)}) async-start(bf16[8,64,128]{2,0,1:T(8,128)(2,1)} %copy.177), calls=%async_computation.4 | async-start | bytes 262144 | tf_op jit(solution)/shard_map/all_to_all | solution.py:215
  302.9 0.9 copy-start.33
  302.9 1.0 copy-start.35
  302.9 84.6 %all-reduce.15.cloned.1.call-start = ((), (), s32[]{:S(2)}) async-start(), calls=%async_computation.14 | async-start | bytes 131072 | tf_op jit(solution)/shard_map/psum | solution.py:226
  303.9 6.5 %copy-start.30 = (f32[8,64,64]{2,1,0:T(8,128)S(1)}, f32[8,64,64]{2,1,0:T(8,128)}, u32[]{:S(2)}) copy-start(f32[8,64,64]{2,1,0:T(8,128)} %get-tuple-element.64) | copy-start | bytes 393220
  305.9 4.5 copy-start.21
  310.5 4.1 copy-start.27
  312.7 0.9 copy-start.11
  313.6 0.8 copy-start.54
  314.7 1.0 copy-start.5
  319.9 134.7 %reduce-scatter.11.cloned.1.call-start = ((), (), s32[]{:S(2)}) async-start(), calls=%async_computation.10 | async-start | bytes 1179648 | tf_op jit(solution)/shard_map/reduce_scatter | solution.py:96
  324.3 0.9 copy-start.18
  324.3 203.3 %all-reduce.17.cloned.1.call-start = ((), (), s32[]{:S(2)}) async-start(), calls=%async_computation.15 | async-start | bytes 262144 | tf_op jit(solution)/shard_map/psum | solution.py:225
  387.6 1.4 copy-start.62
  388.9 0.7 copy-start.61
  389.6 0.7 copy-start.60
  455.8 1.1 copy-start.50
  456.9 0.7 copy-start.59
  457.3 0.9 copy-start.28
  457.3 90.5 %all-reduce.13.cloned.1.call-start = ((), (), s32[]{:S(2)}) async-start(), calls=%async_computation.11 | async-start | bytes 262144 | tf_op jit(solution)/shard_map/psum | solution.py:122
  527.6 1.5 copy-start.51
  547.8 1.4 copy-start.26
  (19 other events, 12.1 us)
Sparse Core Ops, SparseCore 0:
  50.6 8.5 reduce-scatter.12
  130.9 5.7 reduce-scatter.14
  208.9 61.5 reduce-scatter.8
  279.8 14.6 all-reduce.10
  320.0 67.4 all-reduce.14
  391.2 63.3 reduce-scatter.10
  458.7 68.8 all-reduce.16
  530.6 17.1 all-reduce.12
where the time goes:
time: 559 us; the launch traced here: 557 us
  waiting for transfers between devices  259 us (46%)
  blocking collectives  155 us (28%)
  local copies, waits for them, and re-layouts  50.3 us (9%)
  matrix products  29.9 us (5%)
  other arithmetic  26.4 us (5%)
  starting transfers between devices  22 us (4%)
  between operations  14.9 us (3%)
    all_gather x2, blocking collectives, triangle_forward(): remote_all = lax.all_gather(remote_side, 'dap', axis=1, tiled=True)  69.6 us
    psum x1, waiting for transfers between devices, per_device(): lax.psum(dw_out.astype(jnp.bfloat16), 'dap').astype(jnp.float32)  68.6 us
    reduce_scatter x2, waiting for transfers between devices, triangle_backward(): lax.psum_scatter(jnp.einsum('hij,hik->jhk', grad_mixed, local_side, prefe...  63.7 us
    psum x1, waiting for transfers between devices, per_device(): lax.psum(dg_out.astype(jnp.bfloat16), 'dap').astype(jnp.float32)  61.4 us
    psum x1, blocking collectives, per_device(): head_total = lax.psum(d_head, ('dap', 'rep'))  59.6 us
    psum x2, waiting for transfers between devices, triangle_backward(): lax.psum(partial_sum.astype(jnp.bfloat16), 'rep').astype(jnp.float32)  31.8 us
    unnamed x150, local copies, waits for them, and re-layouts  22.6 us
  transfers between devices with their start and end apart: 12, of which 11 were waited for; matrix products, arithmetic and copies ran while one was open for 5% of the time, Pallas kernels for 0%

commit v1 on v0

--- a/solution.py
+++ b/solution.py
@@ -1,6 +1,8 @@
 import jax
 import jax.numpy as jnp
 from jax import lax
+from jax.experimental import pallas as pl
+from jax.experimental.pallas import tpu as pltpu
 from jax.sharding import PartitionSpec as P
 
 H = 128
@@ -243,9 +245,428 @@
     )
 
 
+def gather_part(pair_input, matrices, dap, rep):
+    rows, residues, channels = pair_input.shape
+    half_rows = rows // rep
+    rep_index = lax.axis_index("rep")
+    dap_index = lax.axis_index("dap")
+    own_rows = lax.dynamic_slice_in_dim(pair_input, rep_index * half_rows, half_rows, 0)
+    stack = jnp.stack(matrices)
+    count, depth, width = stack.shape
+    share = depth // dap
+    own_share = lax.dynamic_slice_in_dim(stack, dap_index * share, share, 1)
+    pair_size = half_rows * residues * channels
+    packed = jnp.concatenate(
+        [own_rows.reshape(-1, channels), own_share.reshape(-1, channels)], axis=0
+    )
+    everything = lax.all_gather(packed, ("dap", "rep"), axis=0, tiled=False)
+    split = pair_size // channels
+    pair_all = everything[:, :split].reshape(dap * rows, residues, channels)
+    tail = everything[:, split:].reshape(dap, rep, count, share, width)
+    mats = jnp.transpose(tail, (2, 0, 3, 1, 4)).reshape(count, depth, rep * width)
+    return (pair_all, mats)
+
+
+F32, BF16 = jnp.float32, jnp.bfloat16
+CH = 128
+LANES = 128
+GROUP = 2
+UNROLL = 8
+
+
+def dot(a, b, da=1, db=0):
+    return lax.dot_general(a, b, (((da,), (db,)), ((), ())), preferred_element_type=F32)
+
+
+def sigmoid(v):
+    return 1.0 / (1.0 + jnp.exp(-v))
+
+
+def mean0(v):
+    return jnp.mean(v, axis=0, keepdims=True)
+
+
+def norm0(v):
+    centred = v - mean0(v)
+    inverse = lax.rsqrt(mean0(centred * centred) + epsilon)
+    return (centred * inverse, inverse)
+
+
+def rounded(v):
+    return v.astype(BF16).astype(F32)
+
+
+def plane_load(ref, group, half, channels):
+    tiles = [
+        ref[pl.ds(group * GROUP + t, channels, stride=half), :] for t in range(GROUP)
+    ]
+    return jnp.concatenate(tiles, axis=1)
+
+
+def plane_store(ref, group, half, values):
+    for t in range(GROUP):
+        ref[pl.ds(group * GROUP + t, values.shape[0], stride=half), :] = values[
+            :, t * LANES : (t + 1) * LANES
+        ]
+
+
+def matrix_load(ref, channel, half):
+    packed = ref[pl.ds(pl.multiple_of(channel * half, half), half), :]
+    n = LANES // 2
+    return jnp.concatenate([packed[:, :n], packed[:, n:]], axis=0)
+
+
+def matrix_store(ref, channel, half, values):
+    packed = jnp.concatenate([values[:half], values[half:]], axis=1)
+    ref[pl.ds(pl.multiple_of(channel * half, half), half), :] = packed
+
+
+def over(count, body):
+    def step(index, carry):
+        body(index)
+        return carry
+
+    lax.fori_loop(0, count, step, 0)
+
+
+def over_channels(channels, body):
+    def step(index):
+        for u in range(UNROLL):
+            body(index * UNROLL + u)
+
+    over(channels // UNROLL, step)
+
+
+def part_kernel(
+    place,
+    pair,
+    mats,
+    head,
+    target,
+    target_t,
+    pair_grad,
+    dw_out,
+    dg_out,
+    do_out,
+    dw_in,
+    dg_in,
+    do_in,
+    d_head,
+    down,
+    up,
+    z0,
+    z1,
+    z2,
+    go,
+    p1,
+    p2,
+    y1,
+    y2,
+    a1,
+    b1,
+    x1,
+    a2,
+    b2,
+    x2,
+    lg,
+    acc1,
+    acc2,
+    acc_o1,
+    acc_o2,
+    acc_h,
+):
+    n = pair.shape[0]
+    half = n // 2
+    groups = half // GROUP
+    own_rows = pair_grad.shape[0]
+    width = dg_out.shape[1]
+    bins = head.shape[1]
+    for side in range(2):
+        for q in range(5):
+            square = mats[side * 6 + q]
+            up[side, :, q * CH : (q + 1) * CH] = square
+            down[side, q * CH : (q + 1) * CH, :] = square.astype(F32).T.astype(BF16)
+    out_t1, out_t2 = mats[5], mats[11]
+    out_n1 = out_t1.astype(F32).T.astype(BF16)
+    out_n2 = out_t2.astype(F32).T.astype(BF16)
+    head_n = head[...]
+    head_t = head_n.astype(F32).T.astype(BF16)
+    heads = jnp.concatenate([head_n.astype(F32)] * 2, axis=1).astype(BF16)
+    for ref in (acc1, acc2, acc_o1, acc_o2, acc_h):
+        ref[...] = jnp.zeros_like(ref)
+
+    def project(g, z, side, proj, a, b):
+        hat, _ = norm0(z)
+        p = dot(down[side], hat.astype(BF16))
+        proj[g] = p
+        plane_store(a, g, half, rounded(sigmoid(p[CH : 2 * CH]) * p[:CH]))
+        plane_store(b, g, half, rounded(sigmoid(p[3 * CH : 4 * CH]) * p[2 * CH : 3 * CH]))
+
+    def mix_norm(g, x):
+        v = plane_load(x, g, half, CH)
+        m = mean0(v)
+        s = lax.rsqrt(mean0(v * v) - m * m + epsilon)
+        return ((v - m) * s, s)
+
+    def update(g, z, x, proj, y, out_t):
+        hat, _ = mix_norm(g, x)
+        upd = dot(out_t, hat.astype(BF16))
+        y[g] = upd
+        return rounded(z + sigmoid(proj[g, 4 * CH :, :]) * upd)
+
+    def first(g):
+        tiles = []
+        for t in range(GROUP):
+            row = g * GROUP + t
+            cells = jnp.concatenate([pair[row].astype(F32), pair[row + half].astype(F32)], axis=0)
+            tiles.append(cells.T)
+        z = jnp.concatenate(tiles, axis=1)
+        z0[g] = z
+        project(g, z, 0, p1, a1, b1)
+
+    over(groups, first)
+
+    def mix_one(h):
+        left = matrix_load(a1, h, half).astype(BF16)
+        right = matrix_load(b1, h, half).astype(BF16)
+        matrix_store(x1, h, half, dot(left, right, 1, 1))
+
+    over_channels(CH, mix_one)
+
+    def second(g):
+        z = update(g, z0[g], x1, p1, y1, out_t1)
+        z1[g] = z
+        project(g, z, 1, p2, a2, b2)
+
+    over(groups, second)
+
+    def mix_two(h):
+        left = matrix_load(a2, h, half).T.astype(BF16)
+        right = matrix_load(b2, h, half).astype(BF16)
+        matrix_store(x2, h, half, dot(left, right))
+
+    over_channels(CH, mix_two)
+
+    def third(g):
+        z = update(g, z1[g], x2, p2, y2, out_t2).astype(BF16)
+        z2[g] = z
+        plane_store(lg, g, half, dot(head_t, z))
+
+    over(groups, third)
+
+    def mirror(b):
+        v = matrix_load(lg, b, half)
+        matrix_store(lg, b, half, v + v.T)
+
+    over_channels(bins, mirror)
+
+    def enter(g, grad, x, proj, y, out_n, acc_o):
+        upd = y[g]
+        gate = sigmoid(proj[g, 4 * CH :, :])
+        scaled = grad * gate
+        proj[g, 4 * CH :, :] = scaled * upd * (1.0 - gate)
+        gy = scaled.astype(BF16)
+        hat, s = mix_norm(g, x)
+        acc_o[...] += dot(hat.astype(BF16), gy, 1, 1)
+        gxn = dot(out_n, gy)
+        gx = s * (gxn - mean0(gxn) - hat * mean0(gxn * hat))
+        plane_store(x, g, half, rounded(gx))
+
+    def loss(g):
+        logits = plane_load(lg, g, half, bins)
+        prob = jnp.exp(logits - jnp.log(jnp.sum(jnp.exp(logits), axis=0, keepdims=True)))
+        ids = lax.broadcasted_iota(jnp.int32, logits.shape, 0)
+        hot = (ids == target[g]).astype(F32)
+        hot_t = (ids == target_t[g]).astype(F32)
+        both = jnp.concatenate([prob - hot, prob - hot_t], axis=0).astype(BF16)
+        grad = dot(heads, both)
+        go[g] = grad
+        acc_h[...] += dot(z2[g], both, 1, 1)
+        enter(g, grad, x2, p2, y2, out_n2, acc_o2)
+
+    over(groups, loss)
+
+    def back_two(h):
+        left = matrix_load(a2, h, half).astype(BF16)
+        right = matrix_load(b2, h, half).astype(BF16)
+        gx = matrix_load(x2, h, half).astype(BF16)
+        matrix_store(a2, h, half, dot(right, gx, 1, 1))
+        matrix_store(b2, h, half, dot(left, gx))
+
+    over_channels(CH, back_two)
+
+    def leave(g, z, proj, a, b, side, acc):
+        ga = plane_load(a, g, half, CH)
+        gb = plane_load(b, g, half, CH)
+        sa = sigmoid(proj[g, CH : 2 * CH, :])
+        sb = sigmoid(proj[g, 3 * CH : 4 * CH, :])
+        ta, tb = ga * sa, gb * sb
+        pieces = [
+            ta,
+            ta * proj[g, :CH, :] * (1.0 - sa),
+            tb,
+            tb * proj[g, 2 * CH : 3 * CH, :] * (1.0 - sb),
+            proj[g, 4 * CH :, :],
+        ]
+        gp = jnp.concatenate([v.astype(BF16) for v in pieces], axis=0)
+        hat, inverse = norm0(z)
+        acc[...] += dot(gp, hat.astype(BF16), 1, 1)
+        return (gp, hat, inverse)
+
+    def finish(g, side, grad, gp, hat, inverse):
+        gn = dot(up[side], gp)
+        return grad + inverse * (gn - mean0(gn) - hat * mean0(gn * hat))
+
+    def fourth(g):
+        grad = finish(g, 1, go[g], *leave(g, z1[g], p2, a2, b2, 1, acc2))
+        go[g] = grad
+        enter(g, grad, x1, p1, y1, out_n1, acc_o1)
+
+    over(groups, fourth)
+
+    def back_one(h):
+        left = matrix_load(a1, h, half).astype(BF16)
+        right = matrix_load(b1, h, half).astype(BF16)
+        gx = matrix_load(x1, h, half)
+        matrix_store(a1, h, half, dot(gx.astype(BF16), right))
+        matrix_store(b1, h, half, dot(gx.T.astype(BF16), left))
+
+    over_channels(CH, back_one)
+
+    row = place[0]
+    upper = row // half
+    low = row - upper * half
+    n_lane = LANES // 2
+
+    def last(g):
+        gp, hat, inverse = leave(g, z0[g], p1, a1, b1, 0, acc1)
+
+        @pl.when((g * GROUP >= low) & (g * GROUP < low + own_rows))
+        def _():
+            grad = finish(g, 0, go[g], gp, hat, inverse)
+            for t in range(GROUP):
+                cells = grad[:, t * LANES : (t + 1) * LANES].T
+                chosen = jnp.where(upper == 0, cells[:n_lane], cells[n_lane:])
+                pair_grad[g * GROUP + t - low] = chosen
+
+    over(groups, last)
+
+    scale = 1.0 / n
+    start = pl.multiple_of(place[1], width)
+    for acc, dw, dg in ((acc1, dw_out, dg_out), (acc2, dw_in, dg_in)):
+        for q in range(4):
+            dw[q] = acc[pl.ds(q * CH + start, width), :].T * scale
+        dg[...] = acc[pl.ds(4 * CH + start, width), :].T * scale
+    do_out[...] = acc_o1[pl.ds(start, width), :] * scale
+    do_in[...] = acc_o2[pl.ds(start, width), :] * scale
+    d_head[...] = (acc_h[:, :bins] + acc_h[:, bins:]) * scale
+
+
+def whole_part(dap, rep):
+    def run(
+        pair_input,
+        outgoing_weights,
+        outgoing_gate,
+        outgoing_output,
+        incoming_weights,
+        incoming_gate,
+        incoming_output,
+        distogram_head,
+        distance_bins,
+        chain_index,
+        chain_swap,
+    ):
+        rows, n, _ = pair_input.shape
+        bins = distogram_head.shape[1]
+        width = outgoing_weights.shape[2]
+        matrices = [outgoing_weights[q] for q in range(4)] + [outgoing_gate, outgoing_output.T]
+        matrices += [incoming_weights[q] for q in range(4)] + [incoming_gate, incoming_output.T]
+        pair_all, mats = gather_part(pair_input, matrices, dap, rep)
+        permuted = residue_permutation(chain_index, chain_swap)
+        positions = jnp.arange(n, dtype=jnp.int32)
+        mover = (permuted[:, None] == positions[None, :]).astype(BF16)
+        moved = jnp.einsum(
+            "ia,ab,jb->ij", mover, distance_bins.astype(BF16), mover, preferred_element_type=F32
+        ).astype(jnp.int32)
+        groups = n // 2 // GROUP
+
+        def blocks(values):
+            split = values.reshape(2, groups, GROUP, n)
+            return jnp.transpose(split, (1, 2, 0, 3)).reshape(groups, 1, GROUP * LANES)
+
+        place = jnp.stack([lax.axis_index("dap") * rows, lax.axis_index("rep") * width])
+        shape = jax.ShapeDtypeStruct
+        vmem = pl.BlockSpec(memory_space=pltpu.VMEM)
+        block = GROUP * LANES
+        cells = pltpu.VMEM((groups, CH, block), F32)
+        plane = pltpu.VMEM((CH * n // 2, LANES), F32)
+        projected = pltpu.VMEM((groups, 5 * CH, block), F32)
+        square = pltpu.VMEM((CH, CH), F32)
+        return pl.pallas_call(
+            part_kernel,
+            out_shape=(
+                shape((rows, n, CH), F32),
+                shape((4, CH, width), F32),
+                shape((CH, width), F32),
+                shape((width, CH), F32),
+                shape((4, CH, width), F32),
+                shape((CH, width), F32),
+                shape((width, CH), F32),
+                shape((CH, bins), F32),
+            ),
+            in_specs=[pl.BlockSpec(memory_space=pltpu.SMEM)] + [vmem] * 5,
+            out_specs=tuple([vmem] * 8),
+            scratch_shapes=[
+                pltpu.VMEM((2, 5 * CH, CH), BF16),
+                pltpu.VMEM((2, CH, 5 * CH), BF16),
+                cells,
+                cells,
+                pltpu.VMEM((groups, CH, block), BF16),
+                cells,
+                projected,
+                projected,
+                cells,
+                cells,
+                plane,
+                plane,
+                plane,
+                plane,
+                plane,
+                plane,
+                pltpu.VMEM((bins * n // 2, LANES), F32),
+                pltpu.VMEM((5 * CH, CH), F32),
+                pltpu.VMEM((5 * CH, CH), F32),
+                square,
+                square,
+                square,
+            ],
+            compiler_params=pltpu.CompilerParams(vmem_limit_bytes=60 * 1024 * 1024),
+        )(
+            place.astype(jnp.int32),
+            pair_all,
+            mats,
+            distogram_head,
+            blocks(moved),
+            blocks(moved.T),
+        )
+
+    return run
+
+
 def solution(mesh):
+    dap, rep = mesh.shape["dap"], mesh.shape["rep"]
+
+    def plan(*arrays):
+        residues, channels = arrays[0].shape[1], arrays[0].shape[2]
+        width, bins = arrays[1].shape[2], arrays[7].shape[1]
+        rows = arrays[0].shape[0]
+        small = residues == LANES // 2 and channels == CH and width * rep == CH
+        small = small and bins * 2 == CH and rows % rep == 0 and rows % GROUP == 0
+        small = small and (residues // 2) % rows == 0 and channels % dap == 0
+        return (whole_part(dap, rep) if small else per_device)(*arrays)
+
     return jax.shard_map(
-        per_device,
+        plan,
         mesh=mesh,
         in_specs=(
             P(("groups", "dap"), None, None),

time: 559 us -> 173 us (0.31)
  waiting for transfers between devices: 259 us -> 38.5 us
  blocking collectives: 155 us -> 0 us
  Pallas kernels: 0 us -> 96.1 us
  matrix products: 29.9 us -> 0.31 us
  local copies, waits for them, and re-layouts: 50.3 us -> 21.1 us
  other arithmetic: 26.4 us -> 1.62 us
  starting transfers between devices: 22 us -> 0.04 us
    psum x4 -> x0, waiting for transfers between devices: 162 us -> none  [the longest x1 68.6 us: per_device(): lax.psum(dw_out.astype(jnp.bfloat16), 'dap').astype(jnp.float32)]
    pallas_call x0 -> x1, Pallas kernels: none -> 96.1 us  [run(): pl.pallas_call(part_kernel, out_shape=(shape((rows, n, CH), F32), shape((...]
    all_gather x7 -> x0, blocking collectives: 84.5 us -> none  [the longest x2 69.6 us: triangle_forward(): remote_all = lax.all_gather(remote_side, 'dap', axis=1, tiled=True)]
    psum x5 -> x0, blocking collectives: 70.2 us -> none  [the longest x1 59.6 us: per_device(): head_total = lax.psum(d_head, ('dap', 'rep'))]
    reduce_scatter x2 -> x0, waiting for transfers between devices: 63.7 us -> none  [triangle_backward(): lax.psum_scatter(jnp.einsum('hij,hik->jhk', grad_mixed, local_side, prefe...]
    all_gather x0 -> x1, waiting for transfers between devices: none -> 38.5 us  [gather_part(): everything = lax.all_gather(packed, ('dap', 'rep'), axis=0, tiled=False)]
    dot_general x27 -> x1, matrix products: 29.9 us -> 0.31 us  [run(): jnp.einsum('ia,ab,jb->ij', mover, distance_bins.astype(BF16), mover, pref...]
    all_to_all x4 -> x0, waiting for transfers between devices: 24 us -> none  [the longest x1 7.55 us: per_device(): lax.all_to_all(grad_rows.astype(jnp.bfloat16), 'dap', split_axis=1, conca...]
  transfers between devices with their start and end apart: 12 -> 1, of which waited for: 11 -> 1; matrix products, arithmetic and copies ran while one was open for 5% -> 2% of each run, Pallas kernels for 0% -> 0%
where the time goes in v1:
time: 173 us; the launch traced here: 172 us
  Pallas kernels  96.1 us (56%)
  waiting for transfers between devices  38.5 us (22%)
  local copies, waits for them, and re-layouts  21.1 us (12%)
  between operations  14.2 us (8%)
    pallas_call x1, Pallas kernels, run(): pl.pallas_call(part_kernel, out_shape=(shape((rows, n, CH), F32), shape((...  96.1 us
    all_gather x1, waiting for transfers between devices, gather_part(): everything = lax.all_gather(packed, ('dap', 'rep'), axis=0, tiled=False)  38.5 us
    pallas_call x5, local copies, waits for them, and re-layouts, run(): pl.pallas_call(part_kernel, out_shape=(shape((rows, n, CH), F32), shape((...  8.05 us
    unnamed x16, local copies, waits for them, and re-layouts  4.65 us
  transfers between devices with their start and end apart: 1, of which 1 were waited for; matrix products, arithmetic and copies ran while one was open for 2% of the time, Pallas kernels for 0%

profile of v1, /device:TPU:0, one launch (start us, length us, event | category | flops | bytes accessed | tf_op | source)
XLA Modules:
  0.0 171.9 jit_solution(13234595393166438843)
XLA Ops:
  7.2 0.0 copy-start
  7.2 0.0 copy-start.1
  7.2 0.0 copy-start.2
  7.2 0.0 copy-start.4
  7.2 0.0 copy-start.3
  7.2 0.0 all-gather.3.cloned.1.call-start
  7.3 0.9 constant_dynamic-update-slice_fusion.1
  8.1 0.7 bitcast_dynamic-update-slice_fusion.3
  8.9 0.7 bitcast_dynamic-update-slice_fusion.1
  9.6 0.9 constant_dynamic-update-slice_fusion
  10.4 0.7 bitcast_dynamic-update-slice_fusion.2
  11.2 0.7 bitcast_dynamic-update-slice_fusion
  11.9 0.1 constant_dynamic-slice_fusion
  12.0 0.1 copy.38
  12.1 0.1 reshape.58
  12.3 0.0 copy-done
  12.3 0.6 pad_maximum_fusion
  12.9 0.0 all-gather.3.cloned.1.call-update
  13.0 0.0 copy-done.1
  13.0 0.7 copy.43.head
  13.7 0.0 copy-done.2
  13.7 0.1 convert_reduce_fusion
  13.8 0.0 copy-done.4
  13.8 0.2 select_reduce_fusion.1
  14.0 0.1 select_reduce_fusion.2
  14.1 0.0 copy-done.3
  14.1 0.3 convolution_convert_fusion
  14.5 0.7 reshape.63.target
  15.2 0.1 copy.41
  15.3 0.7 reshape.65.target_t
  16.0 0.6 pad_add_fusion.place
  16.6 38.5 %all-gather.3.cloned.1.call-done = bf16[5632,128]{1,0:T(8,128)(2,1)} async-done(((bf16[352,128]{1,0:T(8,128)(2,1)}), bf16[5632,128]{1,0:T(8,128)(2,1)}) %all-gather.3.cloned.1.call-update) | async-done | bytes 1441808 | tf_op jit(solution)/shard_map/all_gather | solution.py:262
  55.1 2.3 %slice.8 = bf16[16,256,128]{2,1,0:T(8,128)(2,1)} slice(bf16[16,352,128]{2,1,0:T(8,128)(2,1)} %bitcast.28), slice={[0:16], [0:256], [0:128]} | slice | bytes 2097152 | tf_op jit(solution)/shard_map/slice | solution.py:264
  57.4 1.0 slice.9
  58.4 0.3 reshape.60
  58.7 1.1 copy.39
  59.8 1.1 reshape.61.mats
  60.9 96.1 %shard_map.170 = (f32[8,64,128]{2,1,0:T(8,128)}, f32[4,128,64]{2,1,0:T(8,128)}, f32[128,64]{1,0:T(8,128)}, f32[64,128]{1,0:T(8,128)}, f32[4,128,64]{2,1,0:T(8,12...) custom-call(s32[2]{0:T(128)} %pad_add_fusion.place, bf16[64,64,128]{2,1,0:T(8,128)(2,1)} %bitcast.26, ...), custom_call_target="tpu_custom_call" | custom-call | tf_op jit(solution)/shard_map/pallas_call | solution.py:605
  157.0 1.7 %copy.44 = f32[4,128,64]{1,2,0:T(8,128)} copy(f32[4,128,64]{2,1,0:T(8,128)} %get-tuple-element.25) | data formatting | bytes 262144 | tf_op jit(solution)/shard_map/pallas_call | solution.py:605
  158.7 1.5 copy.45
  160.2 1.7 %copy.46 = f32[4,128,64]{1,2,0:T(8,128)} copy(f32[4,128,64]{2,1,0:T(8,128)} %get-tuple-element.28) | data formatting | bytes 262144 | tf_op jit(solution)/shard_map/pallas_call | solution.py:605
  162.0 1.5 copy.47
  163.5 1.5 copy.48
  (4 shorter events, 0.1 us)
Async XLA Ops:
  7.2 5.1 %copy-start = (bf16[8,64,128]{2,1,0:T(8,128)(2,1)S(1)}, bf16[8,64,128]{2,1,0:T(8,128)(2,1)}, u32[]{:S(2)}) copy-start(bf16[8,64,128]{2,1,0:T(8,128)(2,1)} %param.11) | copy-start | bytes 393220
  7.2 5.8 %copy-start.1 = (bf16[128,64]{0,1:T(8,128)(2,1)S(1)}, bf16[128,64]{0,1:T(8,128)(2,1)}, u32[]{:S(2)}) copy-start(bf16[128,64]{0,1:T(8,128)(2,1)} %param.18) | copy-start | bytes 49156
  7.2 6.5 %copy-start.2 = (s32[64]{0:T(128)S(1)}, s32[64]{0:T(128)}, u32[]{:S(2)}) copy-start(s32[64]{0:T(128)} %param.20) | copy-start | bytes 772
  7.2 6.6 %copy-start.4 = (s32[8]{0:T(128)S(1)}, s32[8]{0:T(128)}, u32[]{:S(2)}) copy-start(s32[8]{0:T(128)} %param.21) | copy-start | bytes 100
  7.2 6.9 %copy-start.3 = (s32[64,64]{1,0:T(8,128)S(1)}, s32[64,64]{1,0:T(8,128)}, u32[]{:S(2)}) copy-start(s32[64,64]{1,0:T(8,128)} %param.19) | copy-start | bytes 49156
  7.2 47.9 %all-gather.3.cloned.1.call-start = ((), (), s32[]{:S(2)}) async-start(), calls=%async_computation | async-start | bytes 1531904 | tf_op jit(solution)/shard_map/all_gather | solution.py:262
Sparse Core Ops, SparseCore 0:
  13.1 41.9 all-gather.2

commit v2 on v1

--- a/solution.py
+++ b/solution.py
@@ -1,3 +1,5 @@
+import functools
+
 import jax
 import jax.numpy as jnp
 from jax import lax
@@ -245,28 +247,6 @@
     )
 
 
-def gather_part(pair_input, matrices, dap, rep):
-    rows, residues, channels = pair_input.shape
-    half_rows = rows // rep
-    rep_index = lax.axis_index("rep")
-    dap_index = lax.axis_index("dap")
-    own_rows = lax.dynamic_slice_in_dim(pair_input, rep_index * half_rows, half_rows, 0)
-    stack = jnp.stack(matrices)
-    count, depth, width = stack.shape
-    share = depth // dap
-    own_share = lax.dynamic_slice_in_dim(stack, dap_index * share, share, 1)
-    pair_size = half_rows * residues * channels
-    packed = jnp.concatenate(
-        [own_rows.reshape(-1, channels), own_share.reshape(-1, channels)], axis=0
-    )
-    everything = lax.all_gather(packed, ("dap", "rep"), axis=0, tiled=False)
-    split = pair_size // channels
-    pair_all = everything[:, :split].reshape(dap * rows, residues, channels)
-    tail = everything[:, split:].reshape(dap, rep, count, share, width)
-    mats = jnp.transpose(tail, (2, 0, 3, 1, 4)).reshape(count, depth, rep * width)
-    return (pair_all, mats)
-
-
 F32, BF16 = jnp.float32, jnp.bfloat16
 CH = 128
 LANES = 128
@@ -279,7 +259,7 @@
 
 
 def sigmoid(v):
-    return 1.0 / (1.0 + jnp.exp(-v))
+    return 0.5 * jnp.tanh(0.5 * v) + 0.5
 
 
 def mean0(v):
@@ -343,7 +323,6 @@
     mats,
     head,
     target,
-    target_t,
     pair_grad,
     dw_out,
     dg_out,
@@ -374,24 +353,30 @@
     acc_o1,
     acc_o2,
     acc_h,
+    target_t,
 ):
     n = pair.shape[0]
     half = n // 2
     groups = half // GROUP
     own_rows = pair_grad.shape[0]
-    width = dg_out.shape[1]
-    bins = head.shape[1]
+    width = dg_out.shape[0]
+    bins = head.shape[0]
+    def square(index):
+        return jnp.concatenate([mats[0, index], mats[1, index]], axis=0)
+
+    def turned(values):
+        return values.astype(F32).T.astype(BF16)
+
     for side in range(2):
         for q in range(5):
-            square = mats[side * 6 + q]
-            up[side, :, q * CH : (q + 1) * CH] = square
-            down[side, q * CH : (q + 1) * CH, :] = square.astype(F32).T.astype(BF16)
-    out_t1, out_t2 = mats[5], mats[11]
-    out_n1 = out_t1.astype(F32).T.astype(BF16)
-    out_n2 = out_t2.astype(F32).T.astype(BF16)
-    head_n = head[...]
-    head_t = head_n.astype(F32).T.astype(BF16)
-    heads = jnp.concatenate([head_n.astype(F32)] * 2, axis=1).astype(BF16)
+            matrix = square(side * 6 + q)
+            down[side, q * CH : (q + 1) * CH, :] = matrix
+            up[side, :, q * CH : (q + 1) * CH] = turned(matrix)
+    out_n1, out_n2 = square(5), square(11)
+    out_t1, out_t2 = turned(out_n1), turned(out_n2)
+    head_t = head[...]
+    heads = turned(jnp.concatenate([head_t, head_t], axis=0))
+    target_t[...] = target[...].T
     for ref in (acc1, acc2, acc_o1, acc_o2, acc_h):
         ref[...] = jnp.zeros_like(ref)
 
@@ -472,16 +457,20 @@
         gx = s * (gxn - mean0(gxn) - hat * mean0(gxn * hat))
         plane_store(x, g, half, rounded(gx))
 
+    def lane_row(ref, g):
+        rows = [g * GROUP + t + upper * half for t in range(GROUP) for upper in range(2)]
+        return jnp.concatenate([ref[pl.ds(row, 1), :] for row in rows], axis=1)
+
     def loss(g):
         logits = plane_load(lg, g, half, bins)
         prob = jnp.exp(logits - jnp.log(jnp.sum(jnp.exp(logits), axis=0, keepdims=True)))
-        ids = lax.broadcasted_iota(jnp.int32, logits.shape, 0)
-        hot = (ids == target[g]).astype(F32)
-        hot_t = (ids == target_t[g]).astype(F32)
+        ids = lax.broadcasted_iota(jnp.int32, logits.shape, 0).astype(F32)
+        hot = (ids == lane_row(target, g)).astype(F32)
+        hot_t = (ids == lane_row(target_t, g)).astype(F32)
         both = jnp.concatenate([prob - hot, prob - hot_t], axis=0).astype(BF16)
         grad = dot(heads, both)
         go[g] = grad
-        acc_h[...] += dot(z2[g], both, 1, 1)
+        acc_h[...] += dot(both, z2[g], 1, 1)
         enter(g, grad, x2, p2, y2, out_n2, acc_o2)
 
     over(groups, loss)
@@ -555,11 +544,139 @@
     start = pl.multiple_of(place[1], width)
     for acc, dw, dg in ((acc1, dw_out, dg_out), (acc2, dw_in, dg_in)):
         for q in range(4):
-            dw[q] = acc[pl.ds(q * CH + start, width), :].T * scale
-        dg[...] = acc[pl.ds(4 * CH + start, width), :].T * scale
+            dw[q] = acc[pl.ds(q * CH + start, width), :] * scale
+        dg[...] = acc[pl.ds(4 * CH + start, width), :] * scale
     do_out[...] = acc_o1[pl.ds(start, width), :] * scale
     do_in[...] = acc_o2[pl.ds(start, width), :] * scale
-    d_head[...] = (acc_h[:, :bins] + acc_h[:, bins:]) * scale
+    d_head[...] = (acc_h[:bins] + acc_h[bins:]) * scale
+
+
+def gather_kernel(
+    dap,
+    pair,
+    w_out,
+    g_out,
+    o_out,
+    w_in,
+    g_in,
+    o_in,
+    pair_all,
+    mats,
+    send_sem,
+    recv_sem,
+    send_mats,
+    recv_mats,
+):
+    fars = dap // 2
+    mine, rep = lax.axis_index("dap"), lax.axis_index("rep")
+    far, near = mine // 2, mine % 2
+    size = pair_all.shape[1]
+
+    def origin(step):
+        return lax.rem(far - step + fars, fars)
+
+    def slot(origin_far, origin_near, origin_rep):
+        return (origin_far * 2 + origin_near) * 2 + origin_rep
+
+    along = [{"dap": lax.rem(far + step, fars) * 2 + near, "rep": rep} for step in range(fars)]
+    across = {"dap": far * 2 + 1 - near, "rep": rep}
+    partner = {"dap": mine, "rep": 1 - rep}
+
+    barrier = pltpu.get_barrier_semaphore()
+    peers = along[1:] + [across, partner]
+    for peer in peers:
+        pl.semaphore_signal(barrier, inc=1, device_id=peer, device_id_type=pl.DeviceIdType.MESH)
+
+    own = slot(far, near, rep)
+    pair_all[own] = pair[pl.ds(pl.multiple_of(rep * size, size), size), :]
+    mats[rep, 0:4] = w_out[...]
+    mats[rep, 4] = g_out[...]
+    mats[rep, 5] = o_out[...]
+    mats[rep, 6:10] = w_in[...]
+    mats[rep, 10] = g_in[...]
+    mats[rep, 11] = o_in[...]
+    pl.semaphore_wait(barrier, len(peers))
+
+    started = []
+
+    def send(place, index, device):
+        copy = pltpu.make_async_remote_copy(
+            src_ref=pair_all.at[place],
+            dst_ref=pair_all.at[place],
+            send_sem=send_sem.at[index],
+            recv_sem=recv_sem.at[index],
+            device_id=device,
+            device_id_type=pl.DeviceIdType.MESH,
+        )
+        copy.start()
+        started.append(copy)
+
+    def await_block(place, index, device):
+        pltpu.make_async_remote_copy(
+            src_ref=pair_all.at[place],
+            dst_ref=pair_all.at[place],
+            send_sem=send_sem.at[index],
+            recv_sem=recv_sem.at[index],
+            device_id=device,
+            device_id_type=pl.DeviceIdType.MESH,
+        ).wait_recv()
+
+    near_base = fars
+    rep_base = 2 * fars
+    for step in range(1, fars):
+        send(own, step, along[step])
+    send(own, near_base, across)
+    copy_mats = pltpu.make_async_remote_copy(
+        src_ref=mats.at[rep],
+        dst_ref=mats.at[rep],
+        send_sem=send_mats,
+        recv_sem=recv_mats,
+        device_id=partner,
+        device_id_type=pl.DeviceIdType.MESH,
+    )
+    copy_mats.start()
+    send(own, rep_base, partner)
+    for step in range(1, fars):
+        place = slot(origin(step), near, rep)
+        await_block(place, step, along[step])
+        send(place, near_base + step, across)
+        send(place, rep_base + step, partner)
+    for step in range(fars):
+        place = slot(origin(step), 1 - near, rep)
+        await_block(place, near_base + step, across)
+        send(place, rep_base + fars + step, partner)
+    for step in range(fars):
+        await_block(slot(origin(step), near, 1 - rep), rep_base + step, partner)
+        await_block(slot(origin(step), 1 - near, 1 - rep), rep_base + fars + step, partner)
+    copy_mats.wait_recv()
+    for copy in started:
+        copy.wait_send()
+    copy_mats.wait_send()
+
+
+def gather_part(dap, pair, *matrices):
+    size = pair.shape[0] // 2
+    width = matrices[2].shape[0]
+    fars = dap // 2
+    vmem = pl.BlockSpec(memory_space=pltpu.VMEM)
+    return pl.pallas_call(
+        functools.partial(gather_kernel, dap),
+        out_shape=(
+            jax.ShapeDtypeStruct((dap * 2, size, CH), BF16),
+            jax.ShapeDtypeStruct((2, 12, width, CH), BF16),
+        ),
+        in_specs=[vmem] * 7,
+        out_specs=(vmem, vmem),
+        scratch_shapes=[
+            pltpu.SemaphoreType.DMA((4 * fars,)),
+            pltpu.SemaphoreType.DMA((4 * fars,)),
+            pltpu.SemaphoreType.DMA,
+            pltpu.SemaphoreType.DMA,
+        ],
+        compiler_params=pltpu.CompilerParams(
+            collective_id=0, has_side_effects=True, vmem_limit_bytes=32 * 1024 * 1024
+        ),
+    )(pair, *matrices)
 
 
 def whole_part(dap, rep):
@@ -579,20 +696,23 @@
         rows, n, _ = pair_input.shape
         bins = distogram_head.shape[1]
         width = outgoing_weights.shape[2]
-        matrices = [outgoing_weights[q] for q in range(4)] + [outgoing_gate, outgoing_output.T]
-        matrices += [incoming_weights[q] for q in range(4)] + [incoming_gate, incoming_output.T]
-        pair_all, mats = gather_part(pair_input, matrices, dap, rep)
+        pair_all, mats = gather_part(
+            dap,
+            pair_input.reshape(rows * n, CH),
+            jnp.swapaxes(outgoing_weights, 1, 2),
+            outgoing_gate.T,
+            outgoing_output,
+            jnp.swapaxes(incoming_weights, 1, 2),
+            incoming_gate.T,
+            incoming_output,
+        )
         permuted = residue_permutation(chain_index, chain_swap)
         positions = jnp.arange(n, dtype=jnp.int32)
         mover = (permuted[:, None] == positions[None, :]).astype(BF16)
         moved = jnp.einsum(
             "ia,ab,jb->ij", mover, distance_bins.astype(BF16), mover, preferred_element_type=F32
-        ).astype(jnp.int32)
+        )
         groups = n // 2 // GROUP
-
-        def blocks(values):
-            split = values.reshape(2, groups, GROUP, n)
-            return jnp.transpose(split, (1, 2, 0, 3)).reshape(groups, 1, GROUP * LANES)
 
         place = jnp.stack([lax.axis_index("dap") * rows, lax.axis_index("rep") * width])
         shape = jax.ShapeDtypeStruct
@@ -602,19 +722,19 @@
         plane = pltpu.VMEM((CH * n // 2, LANES), F32)
         projected = pltpu.VMEM((groups, 5 * CH, block), F32)
         square = pltpu.VMEM((CH, CH), F32)
-        return pl.pallas_call(
+        outs = pl.pallas_call(
             part_kernel,
             out_shape=(
                 shape((rows, n, CH), F32),
-                shape((4, CH, width), F32),
-                shape((CH, width), F32),
+                shape((4, width, CH), F32),
                 shape((width, CH), F32),
-                shape((4, CH, width), F32),
-                shape((CH, width), F32),
                 shape((width, CH), F32),
-                shape((CH, bins), F32),
+                shape((4, width, CH), F32),
+                shape((width, CH), F32),
+                shape((width, CH), F32),
+                shape((bins, CH), F32),
             ),
-            in_specs=[pl.BlockSpec(memory_space=pltpu.SMEM)] + [vmem] * 5,
+            in_specs=[pl.BlockSpec(memory_space=pltpu.SMEM)] + [vmem] * 4,
             out_specs=tuple([vmem] * 8),
             scratch_shapes=[
                 pltpu.VMEM((2, 5 * CH, CH), BF16),
@@ -639,15 +759,26 @@
                 square,
                 square,
                 square,
+                pltpu.VMEM((n, n), F32),
             ],
             compiler_params=pltpu.CompilerParams(vmem_limit_bytes=60 * 1024 * 1024),
         )(
             place.astype(jnp.int32),
-            pair_all,
+            pair_all.reshape(dap * rows, n, CH),
             mats,
-            distogram_head,
-            blocks(moved),
-            blocks(moved.T),
+            distogram_head.T,
+            moved,
+        )
+        pair_grad, dw_out, dg_out, do_out, dw_in, dg_in, do_in, d_head = outs
+        return (
+            pair_grad,
+            jnp.swapaxes(dw_out, 1, 2),
+            dg_out.T,
+            do_out,
+            jnp.swapaxes(dw_in, 1, 2),
+            dg_in.T,
+            do_in,
+            d_head.T,
         )
 
     return run
@@ -661,8 +792,8 @@
         width, bins = arrays[1].shape[2], arrays[7].shape[1]
         rows = arrays[0].shape[0]
         small = residues == LANES // 2 and channels == CH and width * rep == CH
-        small = small and bins * 2 == CH and rows % rep == 0 and rows % GROUP == 0
-        small = small and (residues // 2) % rows == 0 and channels % dap == 0
+        small = small and bins * 2 == CH and rep == 2 and dap % 2 == 0 and rows % 2 == 0 and rows % GROUP == 0
+        small = small and (residues // 2) % rows == 0
         return (whole_part(dap, rep) if small else per_device)(*arrays)
 
     return jax.shard_map(

time: 173 us -> 124 us (0.72)
  waiting for transfers between devices: 38.5 us -> 0 us
  Pallas kernels: 96.1 us -> 113 us
  local copies, waits for them, and re-layouts: 21.1 us -> 4.86 us
  between operations: 14.2 us -> 0.7 us
    all_gather x1 -> x0, waiting for transfers between devices: 38.5 us -> none  [gather_part(): everything = lax.all_gather(packed, ('dap', 'rep'), axis=0, tiled=False)]
    pallas_call x0 -> x1, Pallas kernels: none -> 16.4 us  [gather_part(): pl.pallas_call(functools.partial(gather_kernel, dap), out_shape=(jax.Shap...]
    pallas_call x5 -> x0, local copies, waits for them, and re-layouts: 8.05 us -> none  [run(): pl.pallas_call(part_kernel, out_shape=(shape((rows, n, CH), F32), shape((...]
    slice x2 -> x0, local copies, waits for them, and re-layouts: 3.31 us -> none  [the longest x1 2.29 us: gather_part(): pair_all = everything[:, :split].reshape(dap * rows, residues, channels)]
    reshape x6 -> x0, local copies, waits for them, and re-layouts: 2.96 us -> none  [the longest x2 1.4 us: blocks(): return jnp.transpose(split, (1, 2, 0, 3)).reshape(groups, 1, GROUP * LANES)]
    unnamed x16 -> x18, local copies, waits for them, and re-layouts: 4.65 us -> 4.86 us
  transfers between devices with their start and end apart: 1 -> 0, of which waited for: 1 -> 0; matrix products, arithmetic and copies ran while one was open for 2% -> 0% of each run, Pallas kernels for 0% -> 0%
where the time goes in v2:
time: 124 us; the launch traced here: 123 us
  Pallas kernels  113 us (91%)
  local copies, waits for them, and re-layouts  4.86 us (4%)
  other arithmetic  3 us (2%)
  matrix products  1.68 us (1%)
    pallas_call x1, Pallas kernels, run(): pl.pallas_call(part_kernel, out_shape=(shape((rows, n, CH), F32), shape((...  96.5 us
    pallas_call x1, Pallas kernels, gather_part(): pl.pallas_call(functools.partial(gather_kernel, dap), out_shape=(jax.Shap...  16.4 us
    unnamed x18, local copies, waits for them, and re-layouts  4.86 us

profile of v2, /device:TPU:0, one launch (start us, length us, event | category | flops | bytes accessed | tf_op | source)
XLA Modules:
  0.0 123.2 jit_solution(8646957473154945376)
XLA Ops:
  0.6 0.0 copy-start.2
  0.6 0.6 pad_add_fusion.place
  1.3 0.8 convert_reduce_fusion
  2.1 0.8 select_reduce_fusion.1
  2.9 0.7 select_reduce_fusion.2
  3.7 0.0 copy-start.5
  3.7 0.0 copy-start.6
  3.7 1.7 %fusion.target = f32[64,64]{1,0:T(8,128)} fusion(s32[64,64]{1,0:T(8,128)} %param.19, s32[64]{0:T(128)S(1)} %subtract_add_fusion), kind=kOutput, calls=%fused_computation | convolution fusion | flops 1060864 | bytes 33024 | tf_op jit(solution)/shard_map/ia,ab,jb->ij/dot_general | solution.py:712
  5.4 0.0 copy-done.2
  5.4 0.0 copy-done.5
  5.4 0.0 copy-done.6
  5.4 0.0 copy-start.3
  5.4 0.8 copy-done.3
  6.2 0.0 copy-start.4
  6.2 0.8 copy-done.4
  7.1 0.0 copy-start.7
  7.1 0.7 copy-done.7
  7.8 0.0 copy-start.8
  7.8 0.7 copy-done.8
  8.5 16.4 %shard_map.170 = (bf16[16,256,128]{2,1,0:T(8,128)(2,1)S(1)}, bf16[2,12,64,128]{3,2,1,0:T(8,128)(2,1)S(1)}) custom-call(bf16[512,128]{1,0:T(8,128)(2,1)S(1)} %bitcast.15, bf16[4,64,128]{2,1,0:T(8,128)(2,1)S(1)} %bitcast.16, bf16[64,128]{1,0:T(8,128)(2,1)S(1)} %bitcast.18, bf16[64,128]{1,0:T(8,128)(2,1)S(1)} %copy-done.6, bf16[4,64,128]{2,1,0:T(8,128)(2,1)S(1)} %bitcast.17, ...), custom_call_target="tpu_custom_call" | custom-call | tf_op jit(solution)/shard_map/pallas_call | solution.py:662
  24.9 0.0 copy-start
  24.9 1.0 copy-done
  25.9 0.0 copy-start.1
  25.9 0.8 copy-done.1
  26.7 96.5 %shard_map.171 = (f32[8,64,128]{2,1,0:T(8,128)}, f32[4,64,128]{2,1,0:T(8,128)}, f32[64,128]{1,0:T(8,128)}, f32[64,128]{1,0:T(8,128)}, f32[4,64,128]{2,1,0:T(8,12...) custom-call(s32[2]{0:T(128)} %pad_add_fusion.place, bf16[64,64,128]{2,1,0:T(8,128)(2,1)} %bitcast.14, ...), custom_call_target="tpu_custom_call" | custom-call | tf_op jit(solution)/shard_map/pallas_call | solution.py:725
  (1 shorter events, 0.0 us)
Async XLA Ops:
  0.6 4.7 %copy-start.2 = (bf16[8,64,128]{2,1,0:T(8,128)(2,1)S(1)}, bf16[8,64,128]{2,1,0:T(8,128)(2,1)}, u32[]{:S(2)}) copy-start(bf16[8,64,128]{2,1,0:T(8,128)(2,1)} %param.11) | copy-start | bytes 393220
  3.7 1.7 %copy-start.5 = (bf16[128,64]{0,1:T(8,128)(2,1)S(1)}, bf16[128,64]{0,1:T(8,128)(2,1)}, u32[]{:S(2)}) copy-start(bf16[128,64]{0,1:T(8,128)(2,1)} %param.13) | copy-start | bytes 49156
  3.7 1.7 %copy-start.6 = (bf16[64,128]{1,0:T(8,128)(2,1)S(1)}, bf16[64,128]{1,0:T(8,128)(2,1)}, u32[]{:S(2)}) copy-start(bf16[64,128]{1,0:T(8,128)(2,1)} %o_out.1) | copy-start | bytes 49156
  5.4 0.8 copy-start.3
  6.2 0.8 copy-start.4
  7.1 0.7 copy-start.7
  7.8 0.7 copy-start.8
  24.9 1.0 copy-start
  25.9 0.8 copy-start.1

commit v3 on v2

--- a/solution.py
+++ b/solution.py
@@ -251,7 +251,7 @@
 CH = 128
 LANES = 128
 GROUP = 2
-UNROLL = 8
+UNROLL = 32
 
 
 def dot(a, b, da=1, db=0):
@@ -309,10 +309,14 @@
     lax.fori_loop(0, count, step, 0)
 
 
-def over_channels(channels, body):
+def over_channels(channels, half, sources, targets, body):
     def step(index):
-        for u in range(UNROLL):
-            body(index * UNROLL + u)
+        channels_here = [index * UNROLL + u for u in range(UNROLL)]
+        loaded = [[matrix_load(ref, h, half) for ref in sources] for h in channels_here]
+        results = [body(*values) for values in loaded]
+        for h, values in zip(channels_here, results):
+            for ref, value in zip(targets, values):
+                matrix_store(ref, h, half, value)
 
     over(channels // UNROLL, step)
 
@@ -411,12 +415,10 @@
 
     over(groups, first)
 
-    def mix_one(h):
-        left = matrix_load(a1, h, half).astype(BF16)
-        right = matrix_load(b1, h, half).astype(BF16)
-        matrix_store(x1, h, half, dot(left, right, 1, 1))
-
-    over_channels(CH, mix_one)
+    def mix_one(left, right):
+        return (dot(left.astype(BF16), right.astype(BF16), 1, 1),)
+
+    over_channels(CH, half, (a1, b1), (x1,), mix_one)
 
     def second(g):
         z = update(g, z0[g], x1, p1, y1, out_t1)
@@ -425,12 +427,10 @@
 
     over(groups, second)
 
-    def mix_two(h):
-        left = matrix_load(a2, h, half).T.astype(BF16)
-        right = matrix_load(b2, h, half).astype(BF16)
-        matrix_store(x2, h, half, dot(left, right))
-
-    over_channels(CH, mix_two)
+    def mix_two(left, right):
+        return (dot(left.T.astype(BF16), right.astype(BF16)),)
+
+    over_channels(CH, half, (a2, b2), (x2,), mix_two)
 
     def third(g):
         z = update(g, z1[g], x2, p2, y2, out_t2).astype(BF16)
@@ -439,11 +439,10 @@
 
     over(groups, third)
 
-    def mirror(b):
-        v = matrix_load(lg, b, half)
-        matrix_store(lg, b, half, v + v.T)
-
-    over_channels(bins, mirror)
+    def mirror(values):
+        return (values + values.T,)
+
+    over_channels(bins, half, (lg,), (lg,), mirror)
 
     def enter(g, grad, x, proj, y, out_n, acc_o):
         upd = y[g]
@@ -475,14 +474,11 @@
 
     over(groups, loss)
 
-    def back_two(h):
-        left = matrix_load(a2, h, half).astype(BF16)
-        right = matrix_load(b2, h, half).astype(BF16)
-        gx = matrix_load(x2, h, half).astype(BF16)
-        matrix_store(a2, h, half, dot(right, gx, 1, 1))
-        matrix_store(b2, h, half, dot(left, gx))
-
-    over_channels(CH, back_two)
+    def back_two(left, right, grad):
+        gx = grad.astype(BF16)
+        return (dot(right.astype(BF16), gx, 1, 1), dot(left.astype(BF16), gx))
+
+    over_channels(CH, half, (a2, b2, x2), (a2, b2), back_two)
 
     def leave(g, z, proj, a, b, side, acc):
         ga = plane_load(a, g, half, CH)
@@ -513,14 +509,11 @@
 
     over(groups, fourth)
 
-    def back_one(h):
-        left = matrix_load(a1, h, half).astype(BF16)
-        right = matrix_load(b1, h, half).astype(BF16)
-        gx = matrix_load(x1, h, half)
-        matrix_store(a1, h, half, dot(gx.astype(BF16), right))
-        matrix_store(b1, h, half, dot(gx.T.astype(BF16), left))
-
-    over_channels(CH, back_one)
+    def back_one(left, right, gx):
+        ga = dot(gx.astype(BF16), right.astype(BF16))
+        return (ga, dot(gx.T.astype(BF16), left.astype(BF16)))
+
+    over_channels(CH, half, (a1, b1, x1), (a1, b1), back_one)
 
     row = place[0]
     upper = row // half

time: 124 us -> 106 us (0.85)
  Pallas kernels: 113 us -> 95 us
    pallas_call x1, Pallas kernels: 96.5 us -> 78.6 us  [run(): pl.pallas_call(part_kernel, out_shape=(shape((rows, n, CH), F32), shape((...]
where the time goes in v3:
time: 106 us; the launch traced here: 105 us
  Pallas kernels  95 us (90%)
  local copies, waits for them, and re-layouts  4.86 us (5%)
  other arithmetic  3 us (3%)
  matrix products  1.68 us (2%)
    pallas_call x1, Pallas kernels, run(): pl.pallas_call(part_kernel, out_shape=(shape((rows, n, CH), F32), shape((...  78.6 us
    pallas_call x1, Pallas kernels, gather_part(): pl.pallas_call(functools.partial(gather_kernel, dap), out_shape=(jax.Shap...  16.4 us
    unnamed x18, local copies, waits for them, and re-layouts  4.86 us

profile of v3, /device:TPU:0, one launch (start us, length us, event | category | flops | bytes accessed | tf_op | source)
XLA Modules:
  0.0 105.2 jit_solution(4732612258339673726)
XLA Ops:
  0.6 0.0 copy-start.2
  0.6 0.6 pad_add_fusion.place
  1.3 0.8 convert_reduce_fusion
  2.1 0.8 select_reduce_fusion.1
  2.9 0.7 select_reduce_fusion.2
  3.7 0.0 copy-start.5
  3.7 0.0 copy-start.6
  3.7 1.7 %fusion.target = f32[64,64]{1,0:T(8,128)} fusion(s32[64,64]{1,0:T(8,128)} %param.19, s32[64]{0:T(128)S(1)} %subtract_add_fusion), kind=kOutput, calls=%fused_computation | convolution fusion | flops 1060864 | bytes 33024 | tf_op jit(solution)/shard_map/ia,ab,jb->ij/dot_general | solution.py:705
  5.4 0.0 copy-done.2
  5.4 0.0 copy-done.5
  5.4 0.0 copy-done.6
  5.4 0.0 copy-start.3
  5.4 0.8 copy-done.3
  6.2 0.0 copy-start.4
  6.2 0.8 copy-done.4
  7.1 0.0 copy-start.7
  7.1 0.7 copy-done.7
  7.8 0.0 copy-start.8
  7.8 0.7 copy-done.8
  8.5 16.4 %shard_map.170 = (bf16[16,256,128]{2,1,0:T(8,128)(2,1)S(1)}, bf16[2,12,64,128]{3,2,1,0:T(8,128)(2,1)S(1)}) custom-call(bf16[512,128]{1,0:T(8,128)(2,1)S(1)} %bitcast.15, bf16[4,64,128]{2,1,0:T(8,128)(2,1)S(1)} %bitcast.16, bf16[64,128]{1,0:T(8,128)(2,1)S(1)} %bitcast.18, bf16[64,128]{1,0:T(8,128)(2,1)S(1)} %copy-done.6, bf16[4,64,128]{2,1,0:T(8,128)(2,1)S(1)} %bitcast.17, ...), custom_call_target="tpu_custom_call" | custom-call | tf_op jit(solution)/shard_map/pallas_call | solution.py:655
  24.9 0.0 copy-start
  24.9 1.0 copy-done
  25.9 0.0 copy-start.1
  25.9 0.8 copy-done.1
  26.7 78.6 %shard_map.171 = (f32[8,64,128]{2,1,0:T(8,128)}, f32[4,64,128]{2,1,0:T(8,128)}, f32[64,128]{1,0:T(8,128)}, f32[64,128]{1,0:T(8,128)}, f32[4,64,128]{2,1,0:T(8,12...) custom-call(s32[2]{0:T(128)} %pad_add_fusion.place, bf16[64,64,128]{2,1,0:T(8,128)(2,1)} %bitcast.14, ...), custom_call_target="tpu_custom_call" | custom-call | tf_op jit(solution)/shard_map/pallas_call | solution.py:718
  (1 shorter events, 0.0 us)
Async XLA Ops:
  0.6 4.7 %copy-start.2 = (bf16[8,64,128]{2,1,0:T(8,128)(2,1)S(1)}, bf16[8,64,128]{2,1,0:T(8,128)(2,1)}, u32[]{:S(2)}) copy-start(bf16[8,64,128]{2,1,0:T(8,128)(2,1)} %param.11) | copy-start | bytes 393220
  3.7 1.7 %copy-start.5 = (bf16[128,64]{0,1:T(8,128)(2,1)S(1)}, bf16[128,64]{0,1:T(8,128)(2,1)}, u32[]{:S(2)}) copy-start(bf16[128,64]{0,1:T(8,128)(2,1)} %param.13) | copy-start | bytes 49156
  3.7 1.7 %copy-start.6 = (bf16[64,128]{1,0:T(8,128)(2,1)S(1)}, bf16[64,128]{1,0:T(8,128)(2,1)}, u32[]{:S(2)}) copy-start(bf16[64,128]{1,0:T(8,128)(2,1)} %o_out.1) | copy-start | bytes 49156
  5.4 0.8 copy-start.3
  6.2 0.8 copy-start.4
  7.1 0.7 copy-start.7
  7.8 0.7 copy-start.8
  24.9 1.0 copy-start
  25.9 0.8 copy-start.1
